TPU v7x, 32 devices: a whole 2x2x4 slice. The times are simulated.
32 devices in a mesh: groups: 2 (over x), expert: 4 (over y, core), inner: 4 (over z).
Axes of the slice: x: 2, y: 2, z: 4, core: 2. Of those that a mesh axis runs over, the one named last changes fastest.
Arguments:
- quant_rows: bfloat16 [256, 7168], P(('groups', 'expert', 'inner')), parts along dimension 0, may hold values from -4 to 4
- block_scales: bfloat16 [256, 56], P(('groups', 'expert', 'inner')), parts along dimension 0, may hold values from 0.29882812 to 3
- expert_ids: int32 [256, 2], P(('groups', 'expert', 'inner')), parts along dimension 0, may hold values from 0 to 3, all different within a row; in each aligned block of 8 rows (0 to 7, 8 to 15, ...) at most 5 rows name the same one
- gate_scores: float32 [256, 2], P(('groups', 'expert', 'inner')), parts along dimension 0, may hold values from 0.005 to 1
- w_gate: bfloat16 [4, 7168, 2048], P('expert', None, 'inner'), may hold values from -0.0625 to 0.0625
- w_up: bfloat16 [4, 7168, 2048], P('expert', None, 'inner'), may hold values from -0.0625 to 0.0625
- w_down: bfloat16 [4, 2048, 7168], P('expert', 'inner'), may hold values from -0.125 to 0.125
- sketch: bfloat16 [4, 7168, 256], P('expert', 'inner'), may hold values from -0.0625 to 0.0625
- owner_map: int32 [4], replicated, may hold values from 0 to 15, as said below
Outputs:
- mixed: bfloat16 [256, 7168], P(('groups', 'expert', 'inner')), parts along dimension 0
- gram: float32 [32, 256, 256], P(('groups', 'expert', 'inner')), parts along dimension 0
There are 2 independent parts, one for each index of `groups`. A program takes and returns all parts, laid end to end along the dimension named above; an argument that names none is the same for every part. Nothing has to cross between parts.
Inputs may be any that keep to these rules, and one draw needn't show every extreme that they name: `expert_ids`: each token names 2 different experts; in each aligned block of 8 tokens no expert is named by more than 5 tokens, and in every draw some block has an expert named by exactly 5 tokens. `owner_map`: in every draw some expert e has its owner in the group of owners e + 4 // 2 (counted round), groups being 4 consecutive owners.
All inputs are finite; a program needn't handle non-finite values.
Results may differ from a plain program's by a relative error of at most 0.014.
Values may be sent and summed in bfloat16 or wider, within the bound.
A program may use at most 192 MiB of HBM per device.

v0:
```python
import jax
import jax.numpy as jnp
from jax import lax
from jax.sharding import PartitionSpec as P

CAP = 5


def per_device(
    quant_rows, block_scales, expert_ids, gate_scores, w_gate, w_up, w_down, sketch, owner_map
):
    n_expert = lax.axis_size("expert")
    n_inner = lax.axis_size("inner")
    all_blocks = n_expert * n_inner
    tok_count, top_count = expert_ids.shape
    model_width = quant_rows.shape[1]
    scale_cols = block_scales.shape[1]
    experts = owner_map.shape[0]
    sketch_cols = sketch.shape[2]
    total_rows = all_blocks * CAP
    flat_ids = expert_ids.reshape(-1)
    onehot = (flat_ids[:, None] == jnp.arange(experts, dtype=jnp.int32)[None, :]).astype(jnp.int32)
    slot_rank = jnp.sum((jnp.cumsum(onehot, axis=0) - onehot) * onehot, axis=1)
    source_token = jnp.arange(tok_count * top_count, dtype=jnp.int32) // top_count
    slot_table = (
        jnp.full((experts * CAP,), tok_count, jnp.int32)
        .at[flat_ids * CAP + slot_rank]
        .set(source_token)
    )
    padded_rows = jnp.concatenate([quant_rows, jnp.zeros((1, model_width), jnp.bfloat16)], axis=0)
    padded_scales = jnp.concatenate(
        [block_scales, jnp.zeros((1, scale_cols), jnp.bfloat16)], axis=0
    )
    send_rows = padded_rows[slot_table].reshape(experts, CAP, model_width)
    send_scales = padded_scales[slot_table].reshape(experts, CAP, scale_cols)
    wide_rows = jnp.broadcast_to(send_rows[:, None], (experts, n_inner, CAP, model_width))
    wide_scales = jnp.broadcast_to(send_scales[:, None], (experts, n_inner, CAP, scale_cols))
    inner_rows, inner_scales = (
        lax.all_to_all(
            wide_rows.reshape(all_blocks, CAP, model_width),
            ("expert", "inner"),
            split_axis=0,
            concat_axis=0,
            tiled=True,
        ),
        lax.all_to_all(
            wide_scales.reshape(all_blocks, CAP, scale_cols),
            ("expert", "inner"),
            split_axis=0,
            concat_axis=0,
            tiled=True,
        ),
    )
    expanded = inner_rows.reshape(total_rows, scale_cols, model_width // scale_cols).astype(
        jnp.float32
    )
    expanded = expanded * inner_scales.reshape(total_rows, scale_cols, 1).astype(jnp.float32)
    dequant = expanded.reshape(total_rows, model_width).astype(jnp.bfloat16)
    gate_w = w_gate[0]
    up_w = w_up[0]
    down_w = w_down[0]
    gate_proj = jnp.dot(dequant, gate_w, preferred_element_type=jnp.float32)
    up_proj = jnp.dot(dequant, up_w, preferred_element_type=jnp.float32)
    hidden = (jax.nn.silu(gate_proj) * up_proj).astype(jnp.bfloat16)
    partial_value = (
        jnp.dot(hidden, down_w, preferred_element_type=jnp.float32)
        .astype(jnp.bfloat16)
        .reshape(all_blocks, CAP, model_width)
    )
    returned = lax.all_to_all(
        partial_value, ("expert", "inner"), split_axis=0, concat_axis=0, tiled=True
    )
    returned = returned.reshape(n_expert, n_inner, CAP, model_width).astype(jnp.float32)
    outputs = jnp.sum(returned, axis=1).astype(jnp.bfloat16)
    picked = (
        outputs[flat_ids, slot_rank].reshape(tok_count, top_count, model_width).astype(jnp.float32)
    )
    totals = jnp.sum(gate_scores, axis=1, keepdims=True)
    weights = 2.5 * gate_scores / totals
    mixed = jnp.sum(picked * weights[:, :, None], axis=1).astype(jnp.bfloat16)
    part_rows = sketch.shape[1]
    first_col = lax.axis_index("inner") * part_rows
    column_part = lax.dynamic_slice_in_dim(dequant, first_col, part_rows, 1)
    sketched = lax.psum(
        jnp.dot(column_part, sketch[0], preferred_element_type=jnp.float32).astype(jnp.bfloat16),
        "inner",
    ).astype(jnp.float32)
    gram_local = jnp.dot(sketched.T, sketched, precision=lax.Precision.HIGHEST) / (
        tok_count * all_blocks
    )
    gram_all = lax.all_gather(
        gram_local[None].astype(jnp.bfloat16), "expert", axis=0, tiled=True
    ).astype(jnp.float32)
    own_rank = lax.axis_index("expert") * n_inner + lax.axis_index("inner")
    chosen = (owner_map == own_rank).astype(jnp.float32)
    gram_out = jnp.dot(
        chosen[None, :],
        gram_all.reshape(experts, sketch_cols * sketch_cols),
        precision=lax.Precision.HIGHEST,
    ).reshape(1, sketch_cols, sketch_cols)
    return (mixed, gram_out)


def solution(mesh):
    placed = (
        P(("groups", "expert", "inner"), None),
        P(("groups", "expert", "inner"), None),
        P(("groups", "expert", "inner"), None),
        P(("groups", "expert", "inner"), None),
        P("expert", None, "inner"),
        P("expert", None, "inner"),
        P("expert", "inner", None),
        P("expert", "inner", None),
        P(),
    )
    return jax.shard_map(
        per_device,
        mesh=mesh,
        in_specs=placed,
        out_specs=(
            P(("groups", "expert", "inner"), None),
            P(("groups", "expert", "inner"), None, None),
        ),
        check_vma=False,
    )
```

profile of v0, /device:TPU:0, one launch (start us, length us, event | category | flops | bytes accessed | tf_op | source)
XLA Modules:
  0.0 160.3 jit_solution(11582120620384482346)
XLA Ops:
  0.6 0.0 copy-start
  0.6 0.8 copy.17
  1.5 0.1 eq.21
  1.6 0.1 reshape.149
  1.6 0.1 fusion.33
  1.8 0.2 select_reduce_fusion
  2.0 0.6 scatter_custom_fusion
  2.6 0.7 concatenate.10
  3.3 0.6 gather_fusion.1
  3.9 0.7 reshape.198
  4.6 7.4 %all-to-all-start.1 = ((bf16[16,2,140]{2,1,0:T(2,128)(2,1)}), bf16[16,2,140]{2,1,0:T(2,128)(2,1)S(1)}, u32[]{:S(2)}, u32[]{:S(2)}) async-start(bf16[16,2,140]{2,1,0:T(2,128)(2,1)} %reshape.198), calls=%async_computation.1 | async-start | bytes 32768 | tf_op jit(solution)/shard_map/all_to_all | solution.py:46
  12.0 0.9 concatenate.9
  12.9 0.7 gather_fusion
  13.7 0.1 broadcast_in_dim.11
  13.8 4.6 %all-to-all-done.1 = bf16[16,2,140]{2,1,0:T(2,128)(2,1)S(1)} async-done(((bf16[16,2,140]{2,1,0:T(2,128)(2,1)}), bf16[16,2,140]{2,1,0:T(2,128)(2,1)S(1)}, u32[]{:S(2)}, u32[]{:S(2)}) %all-to-all-start.1) | async-done | bytes 8992 | tf_op jit(solution)/shard_map/all_to_all | solution.py:46
  18.4 1.4 broadcast_in_dim.12
  19.9 3.7 %all-to-all-start = ((bf16[16,5,7168]{2,1,0:T(8,128)(2,1)}), bf16[16,5,7168]{2,1,0:T(8,128)(2,1)S(1)}, u32[]{:S(2)}, u32[]{:S(2)}) async-start(bf16[16,5,7168]{2,1,0:T(8,128)(2,1)} %bitcast.62), calls=%async_computation | async-start | bytes 3670016 | tf_op jit(solution)/shard_map/all_to_all | solution.py:39
  23.6 0.1 reshape.199
  23.7 43.7 %all-to-all-done = bf16[16,5,7168]{2,1,0:T(8,128)(2,1)S(1)} async-done(((bf16[16,5,7168]{2,1,0:T(8,128)(2,1)}), bf16[16,5,7168]{2,1,0:T(8,128)(2,1)S(1)}, u32[]{:S(2)}, u32[]{:S(2)}) %all-to-all-start) | async-done | bytes 1146912 | tf_op jit(solution)/shard_map/all_to_all | solution.py:39
  67.4 2.5 %reshape.156 = f32[80,56,128]{2,1,0:T(8,128)} reshape(bf16[16,5,7168]{2,1,0:T(8,128)(2,1)S(1)} %all-to-all-done) | data formatting | bytes 3440640 | tf_op jit(solution)/shard_map/convert_element_type | solution.py:54
  69.9 2.0 %multiply_convert_fusion = bf16[80,56,128]{2,1,0:T(8,128)(2,1)S(1)} fusion(f32[80,56,128]{2,1,0:T(8,128)} %reshape.156, f32[80,56]{1,0:T(8,128)S(1)} %reshape.157), kind=kLoop, calls=%fused_computation.11 | loop fusion | flops 1146880 | bytes 3458560 | tf_op jit(solution)/shard_map/convert_element_type | solution.py:58
  71.9 0.0 copy-start.1
  71.9 1.0 copy-done.1
  72.9 4.5 %fusion.3 = f32[80,512]{1,0:T(8,128)S(1)} fusion(bf16[1,7168,512]{2,1,0:T(8,128)(2,1)} %param.13, bf16[10,8,56,128]{3,2,1,0:T(8,128)(2,1)S(1)} %bitcast.59), kind=kOutput, calls=%fused_computation.8 | convolution fusion | flops 587202560 | bytes 8650752 | tf_op jit(solution)/shard_map/dot_general | solution.py:62
  77.4 9.2 %convolution_convert_fusion = bf16[80,7168]{1,0:T(8,128)(2,1)} fusion(bf16[1,512,7168]{2,1,0:T(8,128)(2,1)} %param.15, bf16[1,7168,512]{2,1,0:T(8,128)(2,1)} %param.14, bf16[10,8,56,128]{3,2,1,0:T(8,128)(2,1)} %bitcast.60, f32[80,512]{1,0:T(8,128)S(1)} %fusion.3), kind=kOutput, calls=%fused_computation.4 | convolution fusion | flops 1175224320 | bytes 17137664 | tf_op jit(solution)/shard_map/dot_general | solution.py:66
  86.6 2.6 %reshape.152 = bf16[16,5,7168]{2,1,0:T(8,128)(2,1)} reshape(bf16[80,7168]{1,0:T(8,128)(2,1)} %convolution_convert_fusion) | data formatting | bytes 2293760 | tf_op jit(solution)/shard_map/reshape | solution.py:68
  89.2 0.0 copy-start.2
  89.2 4.6 %all-to-all-start.2 = ((bf16[16,5,7168]{2,1,0:T(8,128)(2,1)}), bf16[16,5,7168]{2,1,0:T(8,128)(2,1)}, u32[]{:S(2)}, u32[]{:S(2)}) async-start(bf16[16,5,7168]{2,1,0:T(8,128)(2,1)} %reshape.152), calls=%async_computation.2 | async-start | bytes 3670016 | tf_op jit(solution)/shard_map/all_to_all | solution.py:70
  93.8 0.0 copy-done.2
  93.8 0.1 copy.20
  93.9 0.7 mul.63
  94.6 1.8 %copy.36 = f32[10,8,56,128]{3,1,2,0:T(8,128)} copy(f32[10,8,56,128]{3,2,1,0:T(8,128)S(1)} %bitcast.61) | data formatting | bytes 4587520
  96.3 1.6 reshape.159
  97.9 0.0 copy-start.3
  97.9 0.0 copy-done
  97.9 1.5 convolution_convert_fusion.1
  99.5 46.8 %psum.7 = bf16[80,256]{1,0:T(8,128)(2,1)S(1)} all-reduce(bf16[80,256]{1,0:T(8,128)(2,1)S(1)} %convolution_convert_fusion.1), channel_id=1, replica_groups=mesh['groups'=2,'expert'=4,'inner'=4] {'inner'}, use_global_device_ids=true, to_apply=%region_6.7 | all-reduce | flops 20480 | bytes 81920 | tf_op jit(solution)/shard_map/psum | solution.py:84
  146.3 0.2 fusion.5
  146.5 7.3 %all-gather = bf16[1024,256]{1,0:T(8,128)(2,1)S(1)} all-gather(bf16[256,256]{1,0:T(8,128)(2,1)S(1)} %fusion.5), channel_id=2, replica_groups=mesh['groups'=2,'expert'=4,'inner'=4] {'expert'}, dimensions={0}, use_global_device_ids=true | all-gather | bytes 655360 | tf_op jit(solution)/shard_map/all_gather | solution.py:91
  153.8 0.4 reshape.154
  154.2 0.0 copy-done.3
  154.2 0.4 fusion.34
  154.6 0.7 copy.22
  155.3 0.0 all-to-all-done.2
  155.3 1.9 %bitcast_reduce_fusion = bf16[4,5,7168]{2,1,0:T(8,128)(2,1)S(1)} fusion(bf16[16,5,7168]{2,1,0:T(8,128)(2,1)} %all-to-all-done.2), kind=kLoop, calls=%fused_computation.12 | loop fusion | flops 430080 | bytes 1433600 | tf_op jit(solution)/shard_map/reduce_sum | solution.py:74
  157.2 0.3 copy.19
  157.5 1.2 gather_fusion.2
  158.7 0.3 reshape.158
  159.0 1.3 multiply_reduce_fusion
  (10 shorter events, 0.1 us)
Async XLA Ops:
  0.6 97.3 %copy-start = (bf16[1,1792,256]{2,1,0:T(8,128)(2,1)S(1)}, bf16[1,1792,256]{2,1,0:T(8,128)(2,1)}, u32[]{:S(2)}) copy-start(bf16[1,1792,256]{2,1,0:T(8,128)(2,1)} %param.16) | copy-start | bytes 2752516
  4.6 13.8 %all-to-all-start.1 = ((bf16[16,2,140]{2,1,0:T(2,128)(2,1)}), bf16[16,2,140]{2,1,0:T(2,128)(2,1)S(1)}, u32[]{:S(2)}, u32[]{:S(2)}) async-start(bf16[16,2,140]{2,1,0:T(2,128)(2,1)} %reshape.198), calls=%async_computation.1 | async-start | bytes 32768 | tf_op jit(solution)/shard_map/all_to_all | solution.py:46
  19.9 47.5 %all-to-all-start = ((bf16[16,5,7168]{2,1,0:T(8,128)(2,1)}), bf16[16,5,7168]{2,1,0:T(8,128)(2,1)S(1)}, u32[]{:S(2)}, u32[]{:S(2)}) async-start(bf16[16,5,7168]{2,1,0:T(8,128)(2,1)} %bitcast.62), calls=%async_computation | async-start | bytes 3670016 | tf_op jit(solution)/shard_map/all_to_all | solution.py:39
  71.9 1.0 copy-start.1
  89.2 4.6 %copy-start.2 = (f32[8,2]{0,1:T(2,128)S(1)}, f32[8,2]{0,1:T(2,128)}, u32[]{:S(2)}) copy-start(f32[8,2]{0,1:T(2,128)} %param.12) | copy-start | bytes 196
  89.2 66.1 %all-to-all-start.2 = ((bf16[16,5,7168]{2,1,0:T(8,128)(2,1)}), bf16[16,5,7168]{2,1,0:T(8,128)(2,1)}, u32[]{:S(2)}, u32[]{:S(2)}) async-start(bf16[16,5,7168]{2,1,0:T(8,128)(2,1)} %reshape.152), calls=%async_computation.2 | async-start | bytes 3670016 | tf_op jit(solution)/shard_map/all_to_all | solution.py:70
  97.9 56.2 %copy-start.3 = (s32[4]{0:T(128)S(1)}, s32[4]{0:T(128)}, u32[]{:S(2)}) copy-start(s32[4]{0:T(128)} %param.17) | copy-start | bytes 52
where the time goes:
time: 161 us; the launch traced here: 160 us
  blocking collectives  54.1 us (34%)
  waiting for transfers between devices  48.3 us (30%)
  local copies, waits for them, and re-layouts  20 us (12%)
  matrix products  15.8 us (10%)
  starting transfers between devices  15.7 us (10%)
  other arithmetic  5.52 us (3%)
    psum x1, blocking collectives, per_device(): lax.psum(jnp.dot(column_part, sketch[0], preferred_element_type=jnp.float...  46.8 us
    all_to_all x1, waiting for transfers between devices, per_device(): lax.all_to_all(wide_rows.reshape(all_blocks, CAP, model_width), ('expert'...  43.7 us
    dot_general x1, matrix products, per_device(): jnp.dot(hidden, down_w, preferred_element_type=jnp.float32)  9.24 us
    all_to_all x1, starting transfers between devices, per_device(): lax.all_to_all(wide_scales.reshape(all_blocks, CAP, scale_cols), ('expert...  7.39 us
    all_gather x1, blocking collectives, per_device(): lax.all_gather(gram_local[None].astype(jnp.bfloat16), 'expert', axis=0, t...  7.28 us
    all_to_all x1, waiting for transfers between devices, per_device(): lax.all_to_all(wide_scales.reshape(all_blocks, CAP, scale_cols), ('expert...  4.63 us
    all_to_all x1, starting transfers between devices, per_device(): lax.all_to_all(partial_value, ('expert', 'inner'), split_axis=0, concat_a...  4.56 us
    unnamed x12, local copies, waits for them, and re-layouts  4.47 us
  transfers between devices with their start and end apart: 3, of which 2 were waited for; matrix products, arithmetic and copies ran while one was open for 6% of the time, Pallas kernels for 0%

commit v1 on v0

--- a/solution.py
+++ b/solution.py
@@ -1,12 +1,19 @@
+import functools
+
 import jax
 import jax.numpy as jnp
 from jax import lax
+from jax.experimental import pallas as pl
+from jax.experimental.pallas import tpu as pltpu
 from jax.sharding import PartitionSpec as P
 
 CAP = 5
-
-
-def per_device(
+BLOCKS = 2
+LANES = 128
+MESH = pl.DeviceIdType.MESH
+
+
+def exchange_plan(
     quant_rows, block_scales, expert_ids, gate_scores, w_gate, w_up, w_down, sketch, owner_map
 ):
     n_expert = lax.axis_size("expert")
@@ -101,6 +108,538 @@
     return (mixed, gram_out)
 
 
+def layer_kernel(
+    n_inner,
+    experts,
+    quant_ref,
+    scale_ref,
+    ids_ref,
+    score_ref,
+    gate_hbm,
+    up_hbm,
+    down_hbm,
+    sketch_hbm,
+    owner_ref,
+    mixed_ref,
+    gram_ref,
+    gate_w,
+    up_w,
+    down_w,
+    sketch_w,
+    swap_out,
+    swap_in,
+    rows,
+    sk_part,
+    sk_in,
+    sk_all,
+    hidden,
+    own_part,
+    sib_out,
+    sib_in,
+    y_out,
+    y_in,
+    up_out,
+    up_in,
+    dn_out,
+    dn_in,
+    last,
+    last_in,
+    load_sem,
+    swap_sem,
+    zup_s,
+    zup_r,
+    zdn_s,
+    zdn_r,
+    yg_s,
+    yg_r,
+    sg_s,
+    sg_r,
+    skx_s,
+    skx_r,
+    ska_s,
+    ska_r,
+    sib_s,
+    sib_r,
+    yr_s,
+    yr_r,
+    ur_s,
+    ur_r,
+    dr_s,
+    dr_r,
+    last_sem,
+):
+    expert = lax.axis_index("expert")
+    z = lax.axis_index("inner")
+    y, c = expert // 2, expert % 2
+    sibling = {"expert": y * 2 + (1 - c), "inner": z}
+    y_peer = {"expert": (1 - y) * 2 + c, "inner": z}
+    above = {"expert": expert, "inner": lax.rem(z + 1, n_inner)}
+    below = {"expert": expert, "inner": lax.rem(z + n_inner - 1, n_inner)}
+    n_expert = 4
+    devices = n_expert * n_inner
+    chunks = 2 * n_inner
+    tok = quant_ref.shape[0]
+    width = quant_ref.shape[1]
+    half = width // 2
+    blk = width // scale_ref.shape[1]
+    total = chunks * 2 * tok
+    rank = expert * n_inner + z
+
+    def send(src, dst, send_sem, recv_sem, device):
+        return pltpu.make_async_remote_copy(
+            src_ref=src,
+            dst_ref=dst,
+            send_sem=send_sem,
+            recv_sem=recv_sem,
+            device_id=device,
+            device_id_type=MESH,
+        )
+
+    loads = [
+        pltpu.make_async_copy(sketch_hbm.at[0], sketch_w, load_sem.at[0]),
+        pltpu.make_async_copy(gate_hbm.at[0], gate_w, load_sem.at[1]),
+        pltpu.make_async_copy(up_hbm.at[0], up_w, load_sem.at[2]),
+        pltpu.make_async_copy(down_hbm.at[0], down_w, load_sem.at[3]),
+    ]
+
+    barrier = pltpu.get_barrier_semaphore()
+    for step in range(1, devices):
+        other = lax.rem(rank + step, devices)
+        pl.semaphore_signal(
+            barrier,
+            inc=1,
+            device_id={"expert": other // n_inner, "inner": lax.rem(other, n_inner)},
+            device_id_type=MESH,
+        )
+    for load in loads:
+        load.start()
+
+    quant = quant_ref[...].astype(jnp.float32)
+    scales = scale_ref[...].astype(jnp.float32)
+    for j in range(width // blk):
+        part = quant[:, j * blk : (j + 1) * blk] * scales[:, j : j + 1]
+        h, col = divmod(j * blk, half)
+        swap_out[h, :, col : col + blk] = part.astype(jnp.bfloat16).astype(jnp.float32)
+    ids = ids_ref[...]
+    scores = score_ref[...]
+    weights = 2.5 * scores / jnp.sum(scores, axis=1, keepdims=True)
+    lane = lax.broadcasted_iota(jnp.int32, (tok, LANES), 1)
+    meta = jnp.zeros((tok, LANES), jnp.float32)
+    for k in range(ids.shape[1]):
+        named = ids[:, k : k + 1]
+        value = weights[:, k : k + 1]
+        high = value.astype(jnp.bfloat16).astype(jnp.float32)
+        meta = jnp.where(lane == named, high, meta)
+        meta = jnp.where(lane == named + experts, value - high, meta)
+        meta = jnp.where(lane == named + 2 * experts, 1.0, meta)
+    for h in range(2):
+        swap_out[h, :, half:] = meta
+
+    pl.semaphore_wait(barrier, devices - 1)
+
+    swap = send(swap_out.at[1 - c], swap_in, swap_sem.at[0], swap_sem.at[1], sibling)
+    swap.start()
+    swap.wait()
+    mine = y * n_inner + z
+
+    @pl.when(c == 0)
+    def _():
+        rows[0, mine] = jnp.concatenate([swap_out[0], swap_in[...]], axis=0).astype(jnp.bfloat16)
+
+    @pl.when(c == 1)
+    def _():
+        rows[1, mine] = jnp.concatenate([swap_in[...], swap_out[1]], axis=0).astype(jnp.bfloat16)
+
+    def gather_up(src):
+        ref = rows.at[c, y * n_inner + src]
+        return send(ref, ref, zup_s.at[src], zup_r.at[src], above)
+
+    def gather_dn(src):
+        ref = rows.at[c, y * n_inner + src]
+        return send(ref, ref, zdn_s.at[src], zdn_r.at[src], below)
+
+    def gather_y(src):
+        ref = rows.at[c, y * n_inner + src]
+        return send(ref, ref, yg_s.at[src], yg_r.at[src], y_peer)
+
+    def from_y(src):
+        ref = rows.at[c, (1 - y) * n_inner + src]
+        return send(ref, ref, yg_s.at[src], yg_r.at[src], y_peer)
+
+    def gather_sib(chunk):
+        ref = rows.at[c, chunk]
+        return send(ref, ref, sg_s.at[chunk], sg_r.at[chunk], sibling)
+
+    def from_sib(chunk):
+        ref = rows.at[1 - c, chunk]
+        return send(ref, ref, sg_s.at[chunk], sg_r.at[chunk], sibling)
+
+    def when_y(src):
+        from_y(src).wait_recv()
+        gather_sib((1 - y) * n_inner + src).start()
+
+    @pl.when(z < n_inner - 1)
+    def _():
+        gather_up(z).start()
+
+    @pl.when(z > 0)
+    def _():
+        gather_dn(z).start()
+
+    gather_y(z).start()
+    gather_sib(mine).start()
+    for s in range(1, n_inner):
+
+        @pl.when(z - s >= 0)
+        def _():
+            src = lax.rem(z - s + n_inner, n_inner)
+            gather_up(src).wait_recv()
+
+            @pl.when(z < n_inner - 1)
+            def _():
+                gather_up(src).start()
+
+            gather_y(src).start()
+            gather_sib(y * n_inner + src).start()
+
+        @pl.when(z + s < n_inner)
+        def _():
+            src = lax.rem(z + s, n_inner)
+            gather_dn(src).wait_recv()
+
+            @pl.when(z > 0)
+            def _():
+                gather_dn(src).start()
+
+            gather_y(src).start()
+            gather_sib(y * n_inner + src).start()
+
+        if s == 1:
+            when_y(z)
+        else:
+
+            @pl.when(z - s + 1 >= 0)
+            def _():
+                when_y(lax.rem(z - s + 1 + n_inner, n_inner))
+
+            @pl.when(z + s - 1 < n_inner)
+            def _():
+                when_y(lax.rem(z + s - 1, n_inner))
+
+    s = n_inner - 1
+
+    @pl.when(z - s >= 0)
+    def _():
+        when_y(lax.rem(z - s + n_inner, n_inner))
+
+    @pl.when(z + s < n_inner)
+    def _():
+        when_y(lax.rem(z + s, n_inner))
+
+    for chunk in range(chunks):
+        from_sib(chunk).wait_recv()
+
+    info = rows[0, :, :, half:].reshape(total, LANES).astype(jnp.float32)
+    lanes = lax.broadcasted_iota(jnp.int32, (total, LANES), 1)
+
+    def column(index):
+        return jnp.sum(jnp.where(lanes == index, info, 0.0), axis=1, keepdims=True)
+
+    weight = column(expert) + column(expert + experts)
+    routed = column(expert + 2 * experts)
+
+    share = sketch_w.shape[0]
+    per_half = half // share
+    loads[0].wait()
+    start = pl.multiple_of(lax.rem(z, per_half) * share, LANES)
+    columns = rows[z // per_half, :, :, pl.ds(start, share)].reshape(total, share)
+    product = jnp.dot(columns, sketch_w[...], preferred_element_type=jnp.float32) * routed
+    cols = product.shape[1]
+    group = total // n_inner
+    sk_part[...] = product.astype(jnp.bfloat16).reshape(n_inner, group, cols)
+
+    def sk_exchange(step):
+        to = lax.rem(z + step, n_inner)
+        return send(
+            sk_part.at[to],
+            sk_in.at[step],
+            skx_s.at[step],
+            skx_r.at[step],
+            {"expert": expert, "inner": to},
+        )
+
+    for step in range(1, n_inner):
+        sk_exchange(step).start()
+
+    x0 = rows[0, :, :, :half].reshape(total, half)
+    x1 = rows[1, :, :, :half].reshape(total, half)
+    loads[1].wait()
+    loads[2].wait()
+    tile = 256
+
+    def project(n):
+        at = slice(n * tile, (n + 1) * tile)
+        gate = jnp.dot(x0, gate_w[:half, at], preferred_element_type=jnp.float32)
+        gate += jnp.dot(x1, gate_w[half:, at], preferred_element_type=jnp.float32)
+        up = jnp.dot(x0, up_w[:half, at], preferred_element_type=jnp.float32)
+        up += jnp.dot(x1, up_w[half:, at], preferred_element_type=jnp.float32)
+        hidden[:, at] = (gate / (1.0 + jnp.exp(-gate)) * up).astype(jnp.bfloat16)
+
+    tiles = hidden.shape[1] // tile
+    project(0)
+
+    summed = sk_part[z].astype(jnp.float32)
+    for step in range(1, n_inner):
+        sk_exchange(step).wait()
+        summed += sk_in[step].astype(jnp.float32)
+    sk_all[rank] = summed.astype(jnp.bfloat16)
+
+    def sk_gather(step):
+        to = lax.rem(rank + step, devices)
+        return send(
+            sk_all.at[rank],
+            sk_all.at[rank],
+            ska_s.at[step],
+            ska_r.at[step],
+            {"expert": to // n_inner, "inner": lax.rem(to, n_inner)},
+        )
+
+    def sk_arrival(step):
+        origin = lax.rem(rank - step + devices, devices)
+        return send(
+            sk_all.at[origin], sk_all.at[origin], ska_s.at[step], ska_r.at[step], sibling
+        )
+
+    for step in range(1, devices):
+        sk_gather(step).start()
+
+    for n in range(1, tiles):
+        project(n)
+
+    loads[3].wait()
+    blocks, _, _, wide = own_part.shape
+
+    def down(h, b):
+        at = pl.ds(pl.multiple_of(h * half + b * wide, LANES), wide)
+        out = jnp.dot(hidden[...], down_w[:, at], preferred_element_type=jnp.float32)
+        return (out * weight).reshape(chunks, 2 * tok, wide)
+
+    def to_sib(b):
+        return send(sib_out.at[b], sib_in.at[b], sib_s.at[b], sib_r.at[b], sibling)
+
+    def reduce_y(b, dest):
+        return send(y_out.at[b, dest], y_in.at[b, dest], yr_s.at[b, dest], yr_r.at[b, dest], y_peer)
+
+    def reduce_up(b, dest):
+        return send(up_out.at[b, dest], up_in.at[b, dest], ur_s.at[b, dest], ur_r.at[b, dest], above)
+
+    def reduce_dn(b, dest):
+        return send(dn_out.at[b, dest], dn_in.at[b, dest], dr_s.at[b, dest], dr_r.at[b, dest], below)
+
+    def chip_sum(b, y_to, dest):
+        at = y_to * n_inner + dest
+        return own_part[b, at] + sib_in[b, at].astype(jnp.float32)
+
+    order = []
+    for i in range(n_inner // 2):
+        order += [n_inner - 1 - i, i]
+
+    def start_y(b):
+        to_sib(b).wait_recv()
+        for dest in order:
+            y_out[b, dest] = chip_sum(b, 1 - y, dest).astype(jnp.bfloat16)
+            reduce_y(b, dest).start()
+
+    for b in range(blocks):
+        sib_out[b] = down(1 - c, b).astype(jnp.bfloat16)
+        to_sib(b).start()
+        own_part[b] = down(c, b)
+        start_y(b)
+
+    def add_y(b, dest):
+        reduce_y(b, dest).wait_recv()
+        own_part[b, y * n_inner + dest] = chip_sum(b, y, dest) + y_in[b, dest].astype(jnp.float32)
+
+    arrived = set()
+    for i in range(n_inner - 1):
+        for b in range(blocks):
+            top, low = n_inner - 1 - i, i
+            for dest in (top, low):
+                if (b, dest) not in arrived:
+                    arrived.add((b, dest))
+                    add_y(b, dest)
+
+            @pl.when(z < top)
+            def _():
+                up_out[b, top] = own_part[b, y * n_inner + top].astype(jnp.bfloat16)
+
+                @pl.when(z > 0)
+                def _():
+                    reduce_up(b, top).wait_recv()
+                    up_out[b, top] = (
+                        own_part[b, y * n_inner + top] + up_in[b, top].astype(jnp.float32)
+                    ).astype(jnp.bfloat16)
+
+                reduce_up(b, top).start()
+
+            @pl.when(z > low)
+            def _():
+                dn_out[b, low] = own_part[b, y * n_inner + low].astype(jnp.bfloat16)
+
+                @pl.when(z < n_inner - 1)
+                def _():
+                    reduce_dn(b, low).wait_recv()
+                    dn_out[b, low] = (
+                        own_part[b, y * n_inner + low] + dn_in[b, low].astype(jnp.float32)
+                    ).astype(jnp.bfloat16)
+
+                reduce_dn(b, low).start()
+
+    for step in range(1, devices):
+        sk_arrival(step).wait_recv()
+    gram = jnp.zeros((cols, cols), jnp.float32)
+    for e in range(experts):
+        chosen = jnp.where(owner_ref[e] == rank, 1.0 / total, 0.0).astype(jnp.float32)
+        part = sk_all[e * n_inner : (e + 1) * n_inner].reshape(total, cols)
+        gram += chosen * lax.dot_general(
+            part, part, (((0,), (0,)), ((), ())), preferred_element_type=jnp.float32
+        )
+    gram_ref[0] = gram
+
+    for b in range(blocks):
+
+        @pl.when(z > 0)
+        def _():
+            reduce_up(b, z).wait_recv()
+            own_part[b, y * n_inner + z] += up_in[b, z].astype(jnp.float32)
+
+        @pl.when(z < n_inner - 1)
+        def _():
+            reduce_dn(b, z).wait_recv()
+            own_part[b, y * n_inner + z] += dn_in[b, z].astype(jnp.float32)
+
+        done = own_part[b, y * n_inner + z]
+        last[0, b] = done[:tok]
+        last[1, b] = done[tok:]
+    to_last = send(last.at[1 - c], last_in, last_sem.at[0], last_sem.at[1], sibling)
+    to_last.start()
+    to_last.wait()
+    for b in range(blocks):
+        own, other = last[c, b], last_in[b]
+        mixed_ref[:, b * wide : (b + 1) * wide] = jnp.where(c == 0, own, other).astype(jnp.bfloat16)
+        mixed_ref[:, half + b * wide : half + (b + 1) * wide] = jnp.where(
+            c == 0, other, own
+        ).astype(jnp.bfloat16)
+
+    for src in range(n_inner):
+
+        @pl.when((z < n_inner - 1) & (src <= z))
+        def _():
+            gather_up(src).wait_send()
+
+        @pl.when((z > 0) & (src >= z))
+        def _():
+            gather_dn(src).wait_send()
+
+        gather_y(src).wait_send()
+    for chunk in range(chunks):
+        gather_sib(chunk).wait_send()
+    for step in range(1, devices):
+        sk_gather(step).wait_send()
+    for b in range(blocks):
+        to_sib(b).wait_send()
+        for dest in range(n_inner):
+            reduce_y(b, dest).wait_send()
+
+            @pl.when(z < dest)
+            def _():
+                reduce_up(b, dest).wait_send()
+
+            @pl.when(z > dest)
+            def _():
+                reduce_dn(b, dest).wait_send()
+
+
+def gather_plan(
+    quant_rows, block_scales, expert_ids, gate_scores, w_gate, w_up, w_down, sketch, owner_map
+):
+    n_expert = lax.axis_size("expert")
+    n_inner = lax.axis_size("inner")
+    devices = n_expert * n_inner
+    chunks = devices // 2
+    tok, width = quant_rows.shape
+    experts = owner_map.shape[0]
+    half = width // 2
+    rows2 = 2 * tok
+    total = devices * tok
+    units = w_gate.shape[2]
+    share, cols = sketch.shape[1:]
+    group = total // n_inner
+    blocks = BLOCKS
+    wide = half // blocks
+    bf16, f32 = jnp.bfloat16, jnp.float32
+    vmem = pl.BlockSpec(memory_space=pltpu.VMEM)
+    hbm = pl.BlockSpec(memory_space=pl.ANY)
+    dma = pltpu.SemaphoreType.DMA
+    flops = 2 * total * (3 * width * units + share * cols) + 2 * experts * total * cols * cols
+    return pl.pallas_call(
+        functools.partial(layer_kernel, n_inner, experts),
+        out_shape=(
+            jax.ShapeDtypeStruct((tok, width), bf16),
+            jax.ShapeDtypeStruct((1, cols, cols), f32),
+        ),
+        in_specs=[vmem] * 4 + [hbm] * 4 + [pl.BlockSpec(memory_space=pltpu.SMEM)],
+        out_specs=(vmem, vmem),
+        scratch_shapes=[
+            pltpu.VMEM((width, units), bf16),
+            pltpu.VMEM((width, units), bf16),
+            pltpu.VMEM((units, width), bf16),
+            pltpu.VMEM((share, cols), bf16),
+            pltpu.VMEM((2, tok, half + LANES), f32),
+            pltpu.VMEM((tok, half + LANES), f32),
+            pltpu.VMEM((2, chunks, rows2, half + LANES), bf16),
+            pltpu.VMEM((n_inner, group, cols), bf16),
+            pltpu.VMEM((n_inner, group, cols), bf16),
+            pltpu.VMEM((devices, group, cols), bf16),
+            pltpu.VMEM((total, units), bf16),
+            pltpu.VMEM((blocks, chunks, rows2, wide), f32),
+            pltpu.VMEM((blocks, chunks, rows2, wide), bf16),
+            pltpu.VMEM((blocks, chunks, rows2, wide), bf16),
+        ]
+        + [pltpu.VMEM((blocks, n_inner, rows2, wide), bf16)] * 6
+        + [
+            pltpu.VMEM((2, blocks, tok, wide), f32),
+            pltpu.VMEM((blocks, tok, wide), f32),
+            dma((4,)),
+            dma((2,)),
+        ]
+        + [dma((n_inner,))] * 6
+        + [dma((chunks,))] * 2
+        + [dma((n_inner,))] * 2
+        + [dma((devices,))] * 2
+        + [dma((blocks,))] * 2
+        + [dma((blocks, n_inner))] * 6
+        + [dma((2,))],
+        cost_estimate=pl.CostEstimate(
+            flops=flops,
+            bytes_accessed=2 * (3 * width * units + share * cols),
+            transcendentals=total * units,
+        ),
+        compiler_params=pltpu.CompilerParams(
+            collective_id=0, has_side_effects=True, vmem_limit_bytes=56 * 1024 * 1024
+        ),
+    )(quant_rows, block_scales, expert_ids, gate_scores, w_gate, w_up, w_down, sketch, owner_map)
+
+
+def per_device(
+    quant_rows, block_scales, expert_ids, gate_scores, w_gate, w_up, w_down, sketch, owner_map
+):
+    plan = gather_plan if lax.axis_size("expert") == 4 else exchange_plan
+    return plan(
+        quant_rows, block_scales, expert_ids, gate_scores, w_gate, w_up, w_down, sketch, owner_map
+    )
+
+
 def solution(mesh):
     placed = (
         P(("groups", "expert", "inner"), None),

time: 161 us -> 66.7 us (0.41)
  Pallas kernels: 0 us -> 59.9 us
  blocking collectives: 54.1 us -> 0 us
  waiting for transfers between devices: 48.3 us -> 0 us
  matrix products: 15.8 us -> 0 us
  starting transfers between devices: 15.7 us -> 0 us
  local copies, waits for them, and re-layouts: 20 us -> 5.91 us
  other arithmetic: 5.52 us -> 0 us
    pallas_call x0 -> x1, Pallas kernels: none -> 59.9 us  [gather_plan(): pl.pallas_call(functools.partial(layer_kernel, n_inner, experts), out_sha...]
    all_to_all x3 -> x0, waiting for transfers between devices: 48.3 us -> none  [the longest x1 43.7 us: per_device(): lax.all_to_all(wide_rows.reshape(all_blocks, CAP, model_width), ('expert'...]
    psum x1 -> x0, blocking collectives: 46.8 us -> none  [per_device(): lax.psum(jnp.dot(column_part, sketch[0], preferred_element_type=jnp.float...]
    dot_general x5 -> x0, matrix products: 15.8 us -> none  [the longest x1 9.24 us: per_device(): jnp.dot(hidden, down_w, preferred_element_type=jnp.float32)]
    all_to_all x3 -> x0, starting transfers between devices: 15.7 us -> none  [the longest x1 7.39 us: per_device(): lax.all_to_all(wide_scales.reshape(all_blocks, CAP, scale_cols), ('expert...]
    all_gather x1 -> x0, blocking collectives: 7.28 us -> none  [per_device(): lax.all_gather(gram_local[None].astype(jnp.bfloat16), 'expert', axis=0, t...]
    convert_element_type x4 -> x0, local copies, waits for them, and re-layouts: 4.39 us -> none  [the longest x2 4.08 us: per_device(): inner_rows.reshape(total_rows, scale_cols, model_width // scale_cols)]
    reduce_sum x4 -> x0, other arithmetic: 3.36 us -> none  [the longest x1 1.87 us: per_device(): outputs = jnp.sum(returned, axis=1).astype(jnp.bfloat16)]
  transfers between devices with their start and end apart: 3 -> 0, of which waited for: 2 -> 0; matrix products, arithmetic and copies ran while one was open for 6% -> 0% of each run, Pallas kernels for 0% -> 0%
where the time goes in v1:
time: 66.7 us; the launch traced here: 66.4 us
  Pallas kernels  59.9 us (90%)
  local copies, waits for them, and re-layouts  5.91 us (9%)
    pallas_call x1, Pallas kernels, gather_plan(): pl.pallas_call(functools.partial(layer_kernel, n_inner, experts), out_sha...  59.9 us
    unnamed x4, local copies, waits for them, and re-layouts  5.91 us

profile of v1, /device:TPU:0, one launch (start us, length us, event | category | flops | bytes accessed | tf_op | source)
XLA Modules:
  0.0 66.4 jit_solution(10695122111166700425)
XLA Ops:
  0.6 1.3 %copy.11.ids_ref = s32[8,2]{1,0:T(8,128)} copy(s32[8,2]{0,1:T(2,128)} %param.11) | data formatting | bytes 128 | tf_op args[2]
  2.0 1.3 %copy.12.score_ref = f32[8,2]{1,0:T(8,128)} copy(f32[8,2]{0,1:T(2,128)} %param.12) | data formatting | bytes 128 | tf_op args[3]
  3.3 59.9 %shard_map.104 = (bf16[8,7168]{1,0:T(8,128)(2,1)}, f32[1,256,256]{2,1,0:T(8,128)}) custom-call(bf16[8,7168]{1,0:T(8,128)(2,1)} %quant_ref.1, bf16[8,56]{1,0:T(8,128)(2,1)} %scale_ref.1, s32[8,2]{1,0:T(8,128)} %copy.11.ids_ref, f32[8,2]{1,0:T(8,128)} %copy.12.score_ref, bf16[1,7168,512]{2,1,0:T(8,128)(2,1)} %gate_hbm.1, bf16[1,7168,512]{2,1,0:T(8,128)(2,1)} %up_hbm.1, ...), custom_call_target="tpu_custom_call" | custom-call | flops 3003121664 | bytes 22937600 | tf_op jit(solution)/shard_map/pallas_call | solution.py:585
  63.2 1.6 %copy.15 = bf16[8,7168]{1,0:T(8,128)(2,1)} copy(bf16[8,7168]{1,0:T(8,128)(2,1)} %get-tuple-element.4) | data formatting | bytes 229376
  64.8 1.7 %copy.16 = f32[1,256,256]{2,1,0:T(8,128)} copy(f32[1,256,256]{2,1,0:T(8,128)} %get-tuple-element.5) | data formatting | bytes 524288

commit v2 on v1

--- a/solution.py
+++ b/solution.py
@@ -128,7 +128,10 @@
     sketch_w,
     swap_out,
     swap_in,
-    rows,
+    rows_first,
+    rows_second,
+    gate_sum,
+    up_sum,
     sk_part,
     sk_in,
     sk_all,
@@ -138,10 +141,8 @@
     sib_in,
     y_out,
     y_in,
-    up_out,
-    up_in,
-    dn_out,
-    dn_in,
+    z_out,
+    z_in,
     last,
     last_in,
     load_sem,
@@ -158,14 +159,13 @@
     skx_r,
     ska_s,
     ska_r,
+    sky,
     sib_s,
     sib_r,
     yr_s,
     yr_r,
-    ur_s,
-    ur_r,
-    dr_s,
-    dr_r,
+    zr_s,
+    zr_r,
     last_sem,
 ):
     expert = lax.axis_index("expert")
@@ -181,6 +181,8 @@
     tok = quant_ref.shape[0]
     width = quant_ref.shape[1]
     half = width // 2
+    piece = half // 2
+    rows = (rows_first, rows_second)
     blk = width // scale_ref.shape[1]
     total = chunks * 2 * tok
     rank = expert * n_inner + z
@@ -203,14 +205,8 @@
     ]
 
     barrier = pltpu.get_barrier_semaphore()
-    for step in range(1, devices):
-        other = lax.rem(rank + step, devices)
-        pl.semaphore_signal(
-            barrier,
-            inc=1,
-            device_id={"expert": other // n_inner, "inner": lax.rem(other, n_inner)},
-            device_id_type=MESH,
-        )
+    for neighbour in (sibling, y_peer, above, below):
+        pl.semaphore_signal(barrier, inc=1, device_id=neighbour, device_id_type=MESH)
     for load in loads:
         load.start()
 
@@ -220,14 +216,22 @@
         part = quant[:, j * blk : (j + 1) * blk] * scales[:, j : j + 1]
         h, col = divmod(j * blk, half)
         swap_out[h, :, col : col + blk] = part.astype(jnp.bfloat16).astype(jnp.float32)
-    ids = ids_ref[...]
+    ids = ids_ref[...].astype(jnp.float32)
     scores = score_ref[...]
-    weights = 2.5 * scores / jnp.sum(scores, axis=1, keepdims=True)
-    lane = lax.broadcasted_iota(jnp.int32, (tok, LANES), 1)
+    weights = 2.5 * scores / jnp.sum(scores, axis=0, keepdims=True)
+    diagonal = lax.broadcasted_iota(jnp.int32, (tok, tok), 0) == lax.broadcasted_iota(
+        jnp.int32, (tok, tok), 1
+    )
+
+    def upright(row):
+        spread = jnp.where(diagonal, jnp.broadcast_to(row, (tok, tok)), 0.0)
+        return jnp.sum(spread, axis=1, keepdims=True)
+
+    lane = lax.broadcasted_iota(jnp.int32, (tok, LANES), 1).astype(jnp.float32)
     meta = jnp.zeros((tok, LANES), jnp.float32)
-    for k in range(ids.shape[1]):
-        named = ids[:, k : k + 1]
-        value = weights[:, k : k + 1]
+    for k in range(ids.shape[0]):
+        named = upright(ids[k : k + 1])
+        value = upright(weights[k : k + 1])
         high = value.astype(jnp.bfloat16).astype(jnp.float32)
         meta = jnp.where(lane == named, high, meta)
         meta = jnp.where(lane == named + experts, value - high, meta)
@@ -235,111 +239,145 @@
     for h in range(2):
         swap_out[h, :, half:] = meta
 
-    pl.semaphore_wait(barrier, devices - 1)
+    pl.semaphore_wait(barrier, 4)
 
     swap = send(swap_out.at[1 - c], swap_in, swap_sem.at[0], swap_sem.at[1], sibling)
     swap.start()
     swap.wait()
     mine = y * n_inner + z
 
+    def place(h, low, high):
+        pair = jnp.concatenate([low, high], axis=0).astype(jnp.bfloat16)
+        rows[0][h, mine, :, :piece] = pair[:, :piece]
+        rows[0][h, mine, :, piece:] = pair[:, half:]
+        rows[1][h, mine] = pair[:, piece:half]
+
     @pl.when(c == 0)
     def _():
-        rows[0, mine] = jnp.concatenate([swap_out[0], swap_in[...]], axis=0).astype(jnp.bfloat16)
+        place(0, swap_out[0], swap_in[...])
 
     @pl.when(c == 1)
     def _():
-        rows[1, mine] = jnp.concatenate([swap_in[...], swap_out[1]], axis=0).astype(jnp.bfloat16)
-
-    def gather_up(src):
-        ref = rows.at[c, y * n_inner + src]
-        return send(ref, ref, zup_s.at[src], zup_r.at[src], above)
-
-    def gather_dn(src):
-        ref = rows.at[c, y * n_inner + src]
-        return send(ref, ref, zdn_s.at[src], zdn_r.at[src], below)
-
-    def gather_y(src):
-        ref = rows.at[c, y * n_inner + src]
-        return send(ref, ref, yg_s.at[src], yg_r.at[src], y_peer)
-
-    def from_y(src):
-        ref = rows.at[c, (1 - y) * n_inner + src]
-        return send(ref, ref, yg_s.at[src], yg_r.at[src], y_peer)
-
-    def gather_sib(chunk):
-        ref = rows.at[c, chunk]
-        return send(ref, ref, sg_s.at[chunk], sg_r.at[chunk], sibling)
-
-    def from_sib(chunk):
-        ref = rows.at[1 - c, chunk]
-        return send(ref, ref, sg_s.at[chunk], sg_r.at[chunk], sibling)
-
-    def when_y(src):
-        from_y(src).wait_recv()
-        gather_sib((1 - y) * n_inner + src).start()
-
-    @pl.when(z < n_inner - 1)
-    def _():
-        gather_up(z).start()
-
-    @pl.when(z > 0)
-    def _():
-        gather_dn(z).start()
-
-    gather_y(z).start()
-    gather_sib(mine).start()
-    for s in range(1, n_inner):
-
+        place(1, swap_in[...], swap_out[1])
+
+    def gather_up(p, src):
+        ref = rows[p].at[c, y * n_inner + src]
+        return send(ref, ref, zup_s.at[p, src], zup_r.at[p, src], above)
+
+    def gather_dn(p, src):
+        ref = rows[p].at[c, y * n_inner + src]
+        return send(ref, ref, zdn_s.at[p, src], zdn_r.at[p, src], below)
+
+    def gather_y(p, src):
+        ref = rows[p].at[c, y * n_inner + src]
+        return send(ref, ref, yg_s.at[p, src], yg_r.at[p, src], y_peer)
+
+    def from_y(p, src):
+        ref = rows[p].at[c, (1 - y) * n_inner + src]
+        return send(ref, ref, yg_s.at[p, src], yg_r.at[p, src], y_peer)
+
+    def gather_sib(p, chunk):
+        ref = rows[p].at[c, chunk]
+        return send(ref, ref, sg_s.at[p, chunk], sg_r.at[p, chunk], sibling)
+
+    def from_sib(p, chunk):
+        ref = rows[p].at[1 - c, chunk]
+        return send(ref, ref, sg_s.at[p, chunk], sg_r.at[p, chunk], sibling)
+
+    def own(p):
+        @pl.when(z < n_inner - 1)
+        def _():
+            gather_up(p, z).start()
+
+        @pl.when(z > 0)
+        def _():
+            gather_dn(p, z).start()
+
+        gather_y(p, z).start()
+        gather_sib(p, mine).start()
+
+    def z_step(p, s):
         @pl.when(z - s >= 0)
         def _():
             src = lax.rem(z - s + n_inner, n_inner)
-            gather_up(src).wait_recv()
+            gather_up(p, src).wait_recv()
 
             @pl.when(z < n_inner - 1)
             def _():
-                gather_up(src).start()
-
-            gather_y(src).start()
-            gather_sib(y * n_inner + src).start()
+                gather_up(p, src).start()
+
+            gather_y(p, src).start()
+            gather_sib(p, y * n_inner + src).start()
 
         @pl.when(z + s < n_inner)
         def _():
             src = lax.rem(z + s, n_inner)
-            gather_dn(src).wait_recv()
+            gather_dn(p, src).wait_recv()
 
             @pl.when(z > 0)
             def _():
-                gather_dn(src).start()
-
-            gather_y(src).start()
-            gather_sib(y * n_inner + src).start()
-
-        if s == 1:
-            when_y(z)
+                gather_dn(p, src).start()
+
+            gather_y(p, src).start()
+            gather_sib(p, y * n_inner + src).start()
+
+    def when_y(p, src):
+        from_y(p, src).wait_recv()
+        gather_sib(p, (1 - y) * n_inner + src).start()
+
+    def y_step(p, s):
+        if s == 0:
+            when_y(p, z)
+            return
+
+        @pl.when(z - s >= 0)
+        def _():
+            when_y(p, lax.rem(z - s + n_inner, n_inner))
+
+        @pl.when(z + s < n_inner)
+        def _():
+            when_y(p, lax.rem(z + s, n_inner))
+
+    tile = 256
+    tiles = hidden.shape[1] // tile
+
+    def project(p, n):
+        at = slice(n * tile, (n + 1) * tile)
+        sums = []
+        for w in (gate_w, up_w):
+            part = 0.0
+            for h in range(2):
+                x = rows[p][h, :, :, :piece].reshape(total, piece)
+                low = h * half + p * piece
+                part += jnp.dot(x, w[low : low + piece, at], preferred_element_type=jnp.float32)
+            sums.append(part)
+        if p == 0:
+            gate_sum[:, at], up_sum[:, at] = sums
         else:
-
-            @pl.when(z - s + 1 >= 0)
-            def _():
-                when_y(lax.rem(z - s + 1 + n_inner, n_inner))
-
-            @pl.when(z + s - 1 < n_inner)
-            def _():
-                when_y(lax.rem(z + s - 1, n_inner))
-
-    s = n_inner - 1
-
-    @pl.when(z - s >= 0)
-    def _():
-        when_y(lax.rem(z - s + n_inner, n_inner))
-
-    @pl.when(z + s < n_inner)
-    def _():
-        when_y(lax.rem(z + s, n_inner))
-
+            gate, up = gate_sum[:, at] + sums[0], up_sum[:, at] + sums[1]
+            hidden[:, at] = (gate / (1.0 + jnp.exp(-gate)) * up).astype(jnp.bfloat16)
+
+    own(0)
+    own(1)
+    for s in range(1, n_inner):
+        for p in range(2):
+            z_step(p, s)
+    for s in range(n_inner - 1):
+        for p in range(2):
+            y_step(p, s)
+    y_step(0, n_inner - 1)
     for chunk in range(chunks):
-        from_sib(chunk).wait_recv()
-
-    info = rows[0, :, :, half:].reshape(total, LANES).astype(jnp.float32)
+        from_sib(0, chunk).wait_recv()
+    loads[1].wait()
+    loads[2].wait()
+    project(0, 0)
+    y_step(1, n_inner - 1)
+    for n in range(1, tiles):
+        project(0, n)
+    for chunk in range(chunks):
+        from_sib(1, chunk).wait_recv()
+
+    info = rows[0][0, :, :, piece:].reshape(total, LANES).astype(jnp.float32)
     lanes = lax.broadcasted_iota(jnp.int32, (total, LANES), 1)
 
     def column(index):
@@ -348,11 +386,10 @@
     weight = column(expert) + column(expert + experts)
     routed = column(expert + 2 * experts)
 
-    share = sketch_w.shape[0]
-    per_half = half // share
     loads[0].wait()
-    start = pl.multiple_of(lax.rem(z, per_half) * share, LANES)
-    columns = rows[z // per_half, :, :, pl.ds(start, share)].reshape(total, share)
+    h = z // 2
+    columns = jnp.where(lax.rem(z, 2) == 0, rows[0][h, :, :, :piece], rows[1][h])
+    columns = columns.reshape(total, piece)
     product = jnp.dot(columns, sketch_w[...], preferred_element_type=jnp.float32) * routed
     cols = product.shape[1]
     group = total // n_inner
@@ -371,22 +408,7 @@
     for step in range(1, n_inner):
         sk_exchange(step).start()
 
-    x0 = rows[0, :, :, :half].reshape(total, half)
-    x1 = rows[1, :, :, :half].reshape(total, half)
-    loads[1].wait()
-    loads[2].wait()
-    tile = 256
-
-    def project(n):
-        at = slice(n * tile, (n + 1) * tile)
-        gate = jnp.dot(x0, gate_w[:half, at], preferred_element_type=jnp.float32)
-        gate += jnp.dot(x1, gate_w[half:, at], preferred_element_type=jnp.float32)
-        up = jnp.dot(x0, up_w[:half, at], preferred_element_type=jnp.float32)
-        up += jnp.dot(x1, up_w[half:, at], preferred_element_type=jnp.float32)
-        hidden[:, at] = (gate / (1.0 + jnp.exp(-gate)) * up).astype(jnp.bfloat16)
-
-    tiles = hidden.shape[1] // tile
-    project(0)
+    project(1, 0)
 
     summed = sk_part[z].astype(jnp.float32)
     for step in range(1, n_inner):
@@ -394,27 +416,42 @@
         summed += sk_in[step].astype(jnp.float32)
     sk_all[rank] = summed.astype(jnp.bfloat16)
 
-    def sk_gather(step):
-        to = lax.rem(rank + step, devices)
+    def sk_along(step):
         return send(
             sk_all.at[rank],
             sk_all.at[rank],
             ska_s.at[step],
             ska_r.at[step],
-            {"expert": to // n_inner, "inner": lax.rem(to, n_inner)},
+            {"expert": expert, "inner": lax.rem(z + step, n_inner)},
         )
 
-    def sk_arrival(step):
-        origin = lax.rem(rank - step + devices, devices)
-        return send(
-            sk_all.at[origin], sk_all.at[origin], ska_s.at[step], ska_r.at[step], sibling
-        )
-
-    for step in range(1, devices):
-        sk_gather(step).start()
+    def sk_landed(step):
+        ref = sk_all.at[expert * n_inner + lax.rem(z - step + n_inner, n_inner)]
+        return send(ref, ref, ska_s.at[step], ska_r.at[step], sibling)
+
+    def sk_block(of):
+        return sk_all.at[pl.ds(of * n_inner, n_inner)]
+
+    far = (1 - y) * 2 + c
+    twin = y * 2 + 1 - c
+    sk_to_y = send(sk_block(expert), sk_block(expert), sky.at[0], sky.at[1], y_peer)
+    sk_from_y = send(sk_block(far), sk_block(far), sky.at[0], sky.at[1], y_peer)
+    sk_near = send(sk_block(expert), sk_block(expert), sky.at[2], sky.at[3], sibling)
+    sk_from_near = send(sk_block(twin), sk_block(twin), sky.at[2], sky.at[3], sibling)
+    sk_far = send(sk_block(far), sk_block(far), sky.at[4], sky.at[5], sibling)
+    cross = (1 - y) * 2 + 1 - c
+    sk_from_far = send(sk_block(cross), sk_block(cross), sky.at[4], sky.at[5], sibling)
+
+    for step in range(1, n_inner):
+        sk_along(step).start()
 
     for n in range(1, tiles):
-        project(n)
+        project(1, n)
+
+    for step in range(1, n_inner):
+        sk_landed(step).wait_recv()
+    sk_to_y.start()
+    sk_near.start()
 
     loads[3].wait()
     blocks, _, _, wide = own_part.shape
@@ -430,23 +467,25 @@
     def reduce_y(b, dest):
         return send(y_out.at[b, dest], y_in.at[b, dest], yr_s.at[b, dest], yr_r.at[b, dest], y_peer)
 
-    def reduce_up(b, dest):
-        return send(up_out.at[b, dest], up_in.at[b, dest], ur_s.at[b, dest], ur_r.at[b, dest], above)
-
-    def reduce_dn(b, dest):
-        return send(dn_out.at[b, dest], dn_in.at[b, dest], dr_s.at[b, dest], dr_r.at[b, dest], below)
+    def reduce_z(b, step):
+        return send(
+            z_out.at[b, step],
+            z_in.at[b, step],
+            zr_s.at[b, step],
+            zr_r.at[b, step],
+            {"expert": expert, "inner": lax.rem(z + step, n_inner)},
+        )
 
     def chip_sum(b, y_to, dest):
         at = y_to * n_inner + dest
         return own_part[b, at] + sib_in[b, at].astype(jnp.float32)
 
-    order = []
-    for i in range(n_inner // 2):
-        order += [n_inner - 1 - i, i]
+    order = [n_inner // 2] + [s for s in range(1, n_inner) if s != n_inner // 2] + [0]
 
     def start_y(b):
         to_sib(b).wait_recv()
-        for dest in order:
+        for step in order:
+            dest = lax.rem(z + step, n_inner)
             y_out[b, dest] = chip_sum(b, 1 - y, dest).astype(jnp.bfloat16)
             reduce_y(b, dest).start()
 
@@ -456,47 +495,21 @@
         own_part[b] = down(c, b)
         start_y(b)
 
-    def add_y(b, dest):
+    def plane_sum(b, dest):
         reduce_y(b, dest).wait_recv()
-        own_part[b, y * n_inner + dest] = chip_sum(b, y, dest) + y_in[b, dest].astype(jnp.float32)
-
-    arrived = set()
-    for i in range(n_inner - 1):
-        for b in range(blocks):
-            top, low = n_inner - 1 - i, i
-            for dest in (top, low):
-                if (b, dest) not in arrived:
-                    arrived.add((b, dest))
-                    add_y(b, dest)
-
-            @pl.when(z < top)
-            def _():
-                up_out[b, top] = own_part[b, y * n_inner + top].astype(jnp.bfloat16)
-
-                @pl.when(z > 0)
-                def _():
-                    reduce_up(b, top).wait_recv()
-                    up_out[b, top] = (
-                        own_part[b, y * n_inner + top] + up_in[b, top].astype(jnp.float32)
-                    ).astype(jnp.bfloat16)
-
-                reduce_up(b, top).start()
-
-            @pl.when(z > low)
-            def _():
-                dn_out[b, low] = own_part[b, y * n_inner + low].astype(jnp.bfloat16)
-
-                @pl.when(z < n_inner - 1)
-                def _():
-                    reduce_dn(b, low).wait_recv()
-                    dn_out[b, low] = (
-                        own_part[b, y * n_inner + low] + dn_in[b, low].astype(jnp.float32)
-                    ).astype(jnp.bfloat16)
-
-                reduce_dn(b, low).start()
-
-    for step in range(1, devices):
-        sk_arrival(step).wait_recv()
+        return chip_sum(b, y, dest) + y_in[b, dest].astype(jnp.float32)
+
+    for b in range(blocks):
+        for step in order[:-1]:
+            dest = lax.rem(z + step, n_inner)
+            z_out[b, step] = plane_sum(b, dest).astype(jnp.bfloat16)
+            reduce_z(b, step).start()
+        if b == 0:
+            sk_from_y.wait_recv()
+            sk_far.start()
+
+    sk_from_near.wait_recv()
+    sk_from_far.wait_recv()
     gram = jnp.zeros((cols, cols), jnp.float32)
     for e in range(experts):
         chosen = jnp.where(owner_ref[e] == rank, 1.0 / total, 0.0).astype(jnp.float32)
@@ -507,18 +520,10 @@
     gram_ref[0] = gram
 
     for b in range(blocks):
-
-        @pl.when(z > 0)
-        def _():
-            reduce_up(b, z).wait_recv()
-            own_part[b, y * n_inner + z] += up_in[b, z].astype(jnp.float32)
-
-        @pl.when(z < n_inner - 1)
-        def _():
-            reduce_dn(b, z).wait_recv()
-            own_part[b, y * n_inner + z] += dn_in[b, z].astype(jnp.float32)
-
-        done = own_part[b, y * n_inner + z]
+        done = plane_sum(b, z)
+        for step in order[:-1]:
+            reduce_z(b, step).wait_recv()
+            done += z_in[b, step].astype(jnp.float32)
         last[0, b] = done[:tok]
         last[1, b] = done[tok:]
     to_last = send(last.at[1 - c], last_in, last_sem.at[0], last_sem.at[1], sibling)
@@ -531,33 +536,31 @@
             c == 0, other, own
         ).astype(jnp.bfloat16)
 
-    for src in range(n_inner):
-
-        @pl.when((z < n_inner - 1) & (src <= z))
-        def _():
-            gather_up(src).wait_send()
-
-        @pl.when((z > 0) & (src >= z))
-        def _():
-            gather_dn(src).wait_send()
-
-        gather_y(src).wait_send()
-    for chunk in range(chunks):
-        gather_sib(chunk).wait_send()
-    for step in range(1, devices):
-        sk_gather(step).wait_send()
+    for p in range(2):
+        for src in range(n_inner):
+
+            @pl.when((z < n_inner - 1) & (src <= z))
+            def _():
+                gather_up(p, src).wait_send()
+
+            @pl.when((z > 0) & (src >= z))
+            def _():
+                gather_dn(p, src).wait_send()
+
+            gather_y(p, src).wait_send()
+        for chunk in range(chunks):
+            gather_sib(p, chunk).wait_send()
+    for step in range(1, n_inner):
+        sk_along(step).wait_send()
+    sk_to_y.wait_send()
+    sk_near.wait_send()
+    sk_far.wait_send()
     for b in range(blocks):
         to_sib(b).wait_send()
         for dest in range(n_inner):
             reduce_y(b, dest).wait_send()
-
-            @pl.when(z < dest)
-            def _():
-                reduce_up(b, dest).wait_send()
-
-            @pl.when(z > dest)
-            def _():
-                reduce_dn(b, dest).wait_send()
+        for step in range(1, n_inner):
+            reduce_z(b, step).wait_send()
 
 
 def gather_plan(
@@ -597,7 +600,10 @@
             pltpu.VMEM((share, cols), bf16),
             pltpu.VMEM((2, tok, half + LANES), f32),
             pltpu.VMEM((tok, half + LANES), f32),
-            pltpu.VMEM((2, chunks, rows2, half + LANES), bf16),
+            pltpu.VMEM((2, chunks, rows2, half // 2 + LANES), bf16),
+            pltpu.VMEM((2, chunks, rows2, half // 2), bf16),
+            pltpu.VMEM((total, units), f32),
+            pltpu.VMEM((total, units), f32),
             pltpu.VMEM((n_inner, group, cols), bf16),
             pltpu.VMEM((n_inner, group, cols), bf16),
             pltpu.VMEM((devices, group, cols), bf16),
@@ -606,19 +612,19 @@
             pltpu.VMEM((blocks, chunks, rows2, wide), bf16),
             pltpu.VMEM((blocks, chunks, rows2, wide), bf16),
         ]
-        + [pltpu.VMEM((blocks, n_inner, rows2, wide), bf16)] * 6
+        + [pltpu.VMEM((blocks, n_inner, rows2, wide), bf16)] * 4
         + [
             pltpu.VMEM((2, blocks, tok, wide), f32),
             pltpu.VMEM((blocks, tok, wide), f32),
             dma((4,)),
             dma((2,)),
         ]
-        + [dma((n_inner,))] * 6
-        + [dma((chunks,))] * 2
-        + [dma((n_inner,))] * 2
-        + [dma((devices,))] * 2
+        + [dma((2, n_inner))] * 6
+        + [dma((2, chunks))] * 2
+        + [dma((n_inner,))] * 4
+        + [dma((6,))]
         + [dma((blocks,))] * 2
-        + [dma((blocks, n_inner))] * 6
+        + [dma((blocks, n_inner))] * 4
         + [dma((2,))],
         cost_estimate=pl.CostEstimate(
             flops=flops,
@@ -628,13 +634,14 @@
         compiler_params=pltpu.CompilerParams(
             collective_id=0, has_side_effects=True, vmem_limit_bytes=56 * 1024 * 1024
         ),
-    )(quant_rows, block_scales, expert_ids, gate_scores, w_gate, w_up, w_down, sketch, owner_map)
+    )(quant_rows, block_scales, expert_ids.T, gate_scores.T, w_gate, w_up, w_down, sketch, owner_map)
 
 
 def per_device(
     quant_rows, block_scales, expert_ids, gate_scores, w_gate, w_up, w_down, sketch, owner_map
 ):
-    plan = gather_plan if lax.axis_size("expert") == 4 else exchange_plan
+    small = lax.axis_size("expert") == 4 and lax.axis_size("inner") == 4
+    plan = gather_plan if small else exchange_plan
     return plan(
         quant_rows, block_scales, expert_ids, gate_scores, w_gate, w_up, w_down, sketch, owner_map
     )

time: 66.7 us -> 55.1 us (0.83)
  Pallas kernels: 59.9 us -> 51.1 us
  local copies, waits for them, and re-layouts: 5.91 us -> 3.22 us
    pallas_call x1, Pallas kernels: 59.9 us -> 51.1 us  [gather_plan(): pl.pallas_call(functools.partial(layer_kernel, n_inner, experts), out_sha...]
    unnamed x4 -> x2, local copies, waits for them, and re-layouts: 5.91 us -> 3.22 us
where the time goes in v2:
time: 55.1 us; the launch traced here: 54.9 us
  Pallas kernels  51.1 us (93%)
  local copies, waits for them, and re-layouts  3.22 us (6%)
  between operations  0.64 us (1%)
    pallas_call x1, Pallas kernels, gather_plan(): pl.pallas_call(functools.partial(layer_kernel, n_inner, experts), out_sha...  51.1 us
    unnamed x2, local copies, waits for them, and re-layouts  3.22 us

profile of v2, /device:TPU:0, one launch (start us, length us, event | category | flops | bytes accessed | tf_op | source)
XLA Modules:
  0.0 54.9 jit_solution(554298008151203343)
XLA Ops:
  0.6 51.1 %shard_map.104 = (bf16[8,7168]{1,0:T(8,128)(2,1)}, f32[1,256,256]{2,1,0:T(8,128)}) custom-call(bf16[8,7168]{1,0:T(8,128)(2,1)} %quant_ref.1, bf16[8,56]{1,0:T(8,128)(2,1)} %scale_ref.1, s32[2,8]{1,0:T(2,128)} %bitcast.2, f32[2,8]{1,0:T(2,128)} %bitcast.3, bf16[1,7168,512]{2,1,0:T(8,128)(2,1)} %gate_hbm.1, bf16[1,7168,512]{2,1,0:T(8,128)(2,1)} %up_hbm.1, ...), custom_call_target="tpu_custom_call" | custom-call | flops 3003121664 | bytes 22937600 | tf_op jit(solution)/shard_map/pallas_call | solution.py:588
  51.7 1.6 %copy.13 = bf16[8,7168]{1,0:T(8,128)(2,1)} copy(bf16[8,7168]{1,0:T(8,128)(2,1)} %get-tuple-element.4) | data formatting | bytes 229376
  53.3 1.7 %copy.14 = f32[1,256,256]{2,1,0:T(8,128)} copy(f32[1,256,256]{2,1,0:T(8,128)} %get-tuple-element.5) | data formatting | bytes 524288

commit v3 on v2

--- a/solution.py
+++ b/solution.py
@@ -408,7 +408,8 @@
     for step in range(1, n_inner):
         sk_exchange(step).start()
 
-    project(1, 0)
+    for n in range(tiles):
+        project(1, n)
 
     summed = sk_part[z].astype(jnp.float32)
     for step in range(1, n_inner):
@@ -445,14 +446,6 @@
     for step in range(1, n_inner):
         sk_along(step).start()
 
-    for n in range(1, tiles):
-        project(1, n)
-
-    for step in range(1, n_inner):
-        sk_landed(step).wait_recv()
-    sk_to_y.start()
-    sk_near.start()
-
     loads[3].wait()
     blocks, _, _, wide = own_part.shape
 
@@ -494,6 +487,11 @@
         to_sib(b).start()
         own_part[b] = down(c, b)
         start_y(b)
+        if b == 0:
+            for step in range(1, n_inner):
+                sk_landed(step).wait_recv()
+            sk_to_y.start()
+            sk_near.start()
 
     def plane_sum(b, dest):
         reduce_y(b, dest).wait_recv()

time: 55.1 us -> 52.6 us (0.955)
  Pallas kernels: 51.1 us -> 48.6 us
    pallas_call x1, Pallas kernels: 51.1 us -> 48.6 us  [gather_plan(): pl.pallas_call(functools.partial(layer_kernel, n_inner, experts), out_sha...]
where the time goes in v3:
time: 52.6 us; the launch traced here: 52.4 us
  Pallas kernels  48.6 us (92%)
  local copies, waits for them, and re-layouts  3.22 us (6%)
  between operations  0.64 us (1%)
    pallas_call x1, Pallas kernels, gather_plan(): pl.pallas_call(functools.partial(layer_kernel, n_inner, experts), out_sha...  48.6 us
    unnamed x2, local copies, waits for them, and re-layouts  3.22 us

profile of v3, /device:TPU:0, one launch (start us, length us, event | category | flops | bytes accessed | tf_op | source)
XLA Modules:
  0.0 52.4 jit_solution(11157988765653548127)
XLA Ops:
  0.6 48.6 %shard_map.104 = (bf16[8,7168]{1,0:T(8,128)(2,1)}, f32[1,256,256]{2,1,0:T(8,128)}) custom-call(bf16[8,7168]{1,0:T(8,128)(2,1)} %quant_ref.1, bf16[8,56]{1,0:T(8,128)(2,1)} %scale_ref.1, s32[2,8]{1,0:T(2,128)} %bitcast.2, f32[2,8]{1,0:T(2,128)} %bitcast.3, bf16[1,7168,512]{2,1,0:T(8,128)(2,1)} %gate_hbm.1, bf16[1,7168,512]{2,1,0:T(8,128)(2,1)} %up_hbm.1, ...), custom_call_target="tpu_custom_call" | custom-call | flops 3003121664 | bytes 22937600 | tf_op jit(solution)/shard_map/pallas_call | solution.py:586
  49.2 1.6 %copy.13 = bf16[8,7168]{1,0:T(8,128)(2,1)} copy(bf16[8,7168]{1,0:T(8,128)(2,1)} %get-tuple-element.4) | data formatting | bytes 229376
  50.8 1.7 %copy.14 = f32[1,256,256]{2,1,0:T(8,128)} copy(f32[1,256,256]{2,1,0:T(8,128)} %get-tuple-element.5) | data formatting | bytes 524288
